TPU v7x, 512 devices: a whole 4x4x16 slice. The times are simulated.
512 devices in a mesh: nodes: 128 (over z, x, core), feat: 4 (over y).
Axes of the slice: x: 4, y: 4, z: 16, core: 2. Of those that a mesh axis runs over, the one named last changes fastest.
Arguments:
- features: bfloat16 [65536, 128], P(('nodes', 'feat')), may hold values from -6 to 6
- block_vals: bfloat16 [512, 122, 128, 128], P(('nodes', 'feat')), may hold values from -3 to 3
- block_cols: int32 [512, 122], P(('nodes', 'feat')), may hold values from 0 to 127, as said below
- block_counts: int32 [512, 122], P(('nodes', 'feat')), may hold values from 1 to 256
- hub_parts: int32 [2], replicated, may hold values from 0 to 126, as said below
- send_blocks: int32 [512, 128], P(('nodes', 'feat')), may hold values from -1 to 3, as said below
- weight: bfloat16 [128, 256], replicated, may hold values from -0.5 to 0.5
- grad_out: bfloat16 [65536, 256], P(('nodes', 'feat')), may hold values from -0.0234375 to 0.0234375
Outputs:
- layer_out: bfloat16 [65536, 256], P(('nodes', 'feat'))
- weight_grad: float32 [128, 256], replicated
Inputs may be any that keep to these rules, and one draw needn't show every extreme that they name: `hub_parts`: 2 distinct partitions. `block_cols`: slots below 2 hold a block of the row's own partition (0 to 3); the next 8 hold h * 4 + b for block b of partition hub_parts[h], and the hub slots of one device's 1 row blocks together name each of the 8 hub blocks once; the rest hold a partition p, neither the row's own nor a hub, for which send_blocks[p * 4 + f, g] is not -1 (g, f the row's partition and column). Every block that send_blocks names is read by some slot of the receiving device. `send_blocks`: entry [d, q] is -1, or a block of d's partition that d sends to the device of partition q in d's column; it is -1 where q is d's own partition, and in every column where d's partition is a hub. The number of partitions that one device reads from differs from device to device.
All inputs are finite; a program needn't handle non-finite values.
Results may differ from a plain program's by a relative error of at most 0.0057.
Values may be sent and summed in bfloat16 or wider, within the bound.
A program may use at most 64 MiB of HBM per device.

v0:
```python
import jax
import jax.numpy as jnp
from jax import lax
from jax.sharding import PartitionSpec as P

KL = 2
KH = 8


def broadcast(block, axis, owner):
    block = jnp.where(lax.axis_index(axis) == owner, block, jnp.zeros_like(block))
    return lax.psum(block, axis)


def per_device(
    features, block_vals, block_cols, block_counts, hub_parts, send_blocks, weight, grad_out
):
    blocks_here = block_vals.shape[0]
    tile_rows = block_vals.shape[2]
    feat_width = features.shape[1]
    members = lax.axis_size("feat")
    part_size = blocks_here * members
    hub_count = hub_parts.shape[0]
    partition = lax.all_gather(features, "feat", axis=0, tiled=True)
    part_blocks = partition.reshape(part_size, tile_rows, feat_width)

    def spread_whole(position, buffer):
        arrived = broadcast(partition, "nodes", hub_parts[position])
        return lax.dynamic_update_index_in_dim(buffer, arrived, position, 0)

    hub_data = lax.fori_loop(
        0, hub_count, spread_whole, jnp.zeros((hub_count,) + partition.shape, jnp.bfloat16)
    )
    hub_blocks = hub_data.reshape(hub_count * part_size, tile_rows, feat_width)
    chosen = jnp.maximum(send_blocks[0], 0)
    outgoing = jnp.take(part_blocks, chosen, axis=0)
    incoming = lax.all_to_all(outgoing, "nodes", split_axis=0, concat_axis=0, tiled=True)
    near_rows = jnp.take(part_blocks, block_cols[:, :KL], axis=0)
    hub_feats = jnp.take(hub_blocks, block_cols[:, KL : KL + KH], axis=0)
    far_rows = jnp.take(incoming, block_cols[:, KL + KH :], axis=0)
    gathered = jnp.concatenate([near_rows, hub_feats, far_rows], axis=1)
    counts = block_counts.astype(jnp.float32)
    fraction = counts / jnp.sum(counts, axis=1, keepdims=True)
    scaled = (fraction[:, :, None, None] * block_vals.astype(jnp.float32)).astype(jnp.bfloat16)
    hidden = jnp.einsum("bkrc,bkcf->brf", scaled, gathered, preferred_element_type=jnp.float32)
    hidden = hidden.reshape(blocks_here * tile_rows, feat_width).astype(jnp.bfloat16)
    layer_out = jnp.dot(hidden, weight, preferred_element_type=jnp.float32).astype(jnp.bfloat16)
    grad_term = lax.dot_general(
        hidden, grad_out, (((0,), (0,)), ((), ())), preferred_element_type=jnp.float32
    )
    weight_grad = lax.psum(grad_term, ("nodes", "feat"))
    return (layer_out, weight_grad)


def solution(mesh):
    placed = (
        P(("nodes", "feat"), None),
        P(("nodes", "feat"), None, None, None),
        P(("nodes", "feat"), None),
        P(("nodes", "feat"), None),
        P(),
        P(("nodes", "feat"), None),
        P(),
        P(("nodes", "feat"), None),
    )
    return jax.shard_map(
        per_device,
        mesh=mesh,
        in_specs=placed,
        out_specs=(P(("nodes", "feat"), None), P()),
        check_vma=False,
    )
```

profile of v0, /device:TPU:1, one launch (start us, length us, event | category | flops | bytes accessed | tf_op | source)
XLA Modules:
  0.0 1200.1 jit_solution(363600921139192560)
XLA Ops:
  8.0 0.0 copy-start
  8.0 0.7 maximum_bitcast_fusion.6
  8.7 0.7 compare_bitcast_fusion
  9.4 10.7 all_gather.3
  20.0 3.1 gather_fusion.2
  23.1 4.6 broadcast_select_fusion
  27.7 0.0 copy-start.4
  27.7 0.0 copy-start.3
  27.7 23.0 %all-to-all-start = ((bf16[128,128,128]{2,1,0:T(8,128)(2,1)}), bf16[128,128,128]{2,1,0:T(8,128)(2,1)}, u32[]{:S(2)}, u32[]{:S(2)}) async-start(bf16[128,128,128]{2,1,0:T(8,128)(2,1)} %broadcast_select_fusion), calls=%async_computation | async-start | bytes 8388608 | tf_op jit(solution)/shard_map/all_to_all | solution.py:37
  50.7 0.0 copy-start.5
  50.8 0.0 copy-done.4
  50.8 0.6 gather_fusion
  51.4 0.1 fusion.16
  51.5 0.0 copy-done.3
  51.5 684.9 %while.13 = (s32[]{:T(128)}, bf16[2,512,128]{2,1,0:T(8,128)(2,1)S(1)}, s32[2]{0:T(128)S(1)}, bf16[512,128]{1,0:T(8,128)(2,1)S(1)}, s32[]{:T(128)}, /*index=5*/u32[]{:T(128)}, u32[]{:T(128)}) while((s32[]{:T(128)}, bf16[2,512,128]{2,1,0:T(8,128)(2,1)S(1)}, s32[2]{0:T(128)S(1)}, bf16[512,128]{1,0:T(8,128)(2,1)S(1)}, s32[]{:T(128)}, ...), condition=%wide.region_3.4_spmd, body=%wide.region_1.3_spmd.sunk | while | flops 131078 | bytes 1310903 | solution.py:31
  51.5 0.0 all-reduce.5.cloned.1.call-start
  51.5 0.6 dynamic_slice.8
  52.8 0.7 select_bitcast_fusion.2
  53.4 0.0 all-reduce.5.cloned.1.call-update
  53.5 364.6 %all-reduce.5.cloned.1.call-done = bf16[1,512,128]{2,1,0:T(8,128)(2,1)} async-done(((bf16[1,512,128]{2,1,0:T(8,128)(2,1)}), bf16[1,512,128]{2,1,0:T(8,128)(2,1)}) %all-reduce.5.cloned.1.call-update) | async-done | bytes 131088 | tf_op jit(solution)/shard_map/while/body/eval_jaxpr/psum | solution.py:12
  418.1 0.9 constant_dynamic-update-slice_fusion.2
  419.0 0.0 all-reduce.5.cloned.1.call-start
  419.1 0.6 dynamic_slice.8
  420.3 0.7 select_bitcast_fusion.2
  421.0 0.0 all-reduce.5.cloned.1.call-update
  421.0 314.4 %all-reduce.5.cloned.1.call-done = bf16[1,512,128]{2,1,0:T(8,128)(2,1)} async-done(((bf16[1,512,128]{2,1,0:T(8,128)(2,1)}), bf16[1,512,128]{2,1,0:T(8,128)(2,1)}) %all-reduce.5.cloned.1.call-update) | async-done | bytes 131088 | tf_op jit(solution)/shard_map/while/body/eval_jaxpr/psum | solution.py:12
  735.4 0.9 constant_dynamic-update-slice_fusion.2
  736.3 0.0 all-reduce.3.cloned.1.call-start
  736.4 0.6 gather_fusion.1
  737.0 0.0 copy-done.5
  737.0 0.6 convert_reduce_fusion
  737.6 0.1 fusion.17
  737.7 0.1 and_bitcast_fusion
  737.8 0.1 and_bitcast_fusion.1
  737.9 0.6 divide_bitcast_fusion
  738.5 0.1 bitcast_select_fusion.2
  738.6 0.1 bitcast_select_fusion.1
  738.7 0.0 all-to-all-done
  738.7 5.1 gather_fusion.3
  743.8 0.0 copy-start.2
  743.8 2.6 bitcast_select_fusion
  746.4 0.6 copy-done.2
  747.0 0.0 copy-start.1
  747.0 1.5 fusion.11
  748.5 0.0 copy-done
  748.5 0.9 fusion.18
  749.4 0.0 all-reduce.3.cloned.1.call-update
  749.4 0.0 copy-done.1
  749.4 0.8 convolution_convert_fusion
  750.2 440.9 %all-reduce.3.cloned.1.call-done = f32[128,256]{1,0:T(8,128)} async-done(((f32[128,256]{1,0:T(8,128)}), f32[128,256]{1,0:T(8,128)}) %all-reduce.3.cloned.1.call-update) | async-done | bytes 131088 | tf_op jit(solution)/shard_map/psum | solution.py:51
  1191.1 1.6 copy.21
  (7 shorter events, 0.0 us)
Async XLA Ops:
  8.0 740.5 %copy-start = (bf16[128,256]{1,0:T(8,128)(2,1)S(1)}, bf16[128,256]{1,0:T(8,128)(2,1)}, u32[]{:S(2)}) copy-start(bf16[128,256]{1,0:T(8,128)(2,1)} %param.17) | copy-start | bytes 196612
  27.7 23.1 %copy-start.4 = (s32[1,122]{1,0:T(1,128)S(1)}, s32[1,122]{1,0:T(1,128)}, u32[]{:S(2)}) copy-start(s32[1,122]{1,0:T(1,128)} %param.12) | copy-start | bytes 1468
  27.7 23.8 %copy-start.3 = (s32[2]{0:T(128)S(1)}, s32[2]{0:T(128)}, u32[]{:S(2)}) copy-start(s32[2]{0:T(128)} %param.14) | copy-start | bytes 28
  27.7 711.0 %all-to-all-start = ((bf16[128,128,128]{2,1,0:T(8,128)(2,1)}), bf16[128,128,128]{2,1,0:T(8,128)(2,1)}, u32[]{:S(2)}, u32[]{:S(2)}) async-start(bf16[128,128,128]{2,1,0:T(8,128)(2,1)} %broadcast_select_fusion), calls=%async_computation | async-start | bytes 8388608 | tf_op jit(solution)/shard_map/all_to_all | solution.py:37
  50.7 686.3 %copy-start.5 = (s32[1,122]{1,0:T(1,128)S(1)}, s32[1,122]{1,0:T(1,128)}, u32[]{:S(2)}) copy-start(s32[1,122]{1,0:T(1,128)} %param.13) | copy-start | bytes 1468
  51.5 366.6 %all-reduce.5.cloned.1.call-start = ((), (), s32[]{:S(2)}) async-start(), calls=%async_computation.2 | async-start | bytes 262144 | tf_op jit(solution)/shard_map/while/body/eval_jaxpr/psum | solution.py:12
  419.0 316.4 %all-reduce.5.cloned.1.call-start = ((), (), s32[]{:S(2)}) async-start(), calls=%async_computation.2 | async-start | bytes 262144 | tf_op jit(solution)/shard_map/while/body/eval_jaxpr/psum | solution.py:12
  736.3 454.7 %all-reduce.3.cloned.1.call-start = ((), (), s32[]{:S(2)}) async-start(), calls=%async_computation.1 | async-start | bytes 262144 | tf_op jit(solution)/shard_map/psum | solution.py:51
  743.8 3.2 copy-start.2
  747.0 2.4 copy-start.1
Sparse Core Ops, SparseCore 0:
  56.7 361.3 all-reduce.4
  424.3 311.0 all-reduce.4
Sparse Core Ops, SparseCore 1:
  749.5 441.6 all-reduce.2
where the time goes:
time: 1200 us
  waiting for transfers between devices  1120 us (93%)
  starting transfers between devices  23.2 us (2%)
  between operations  15.6 us (1%)
  local copies, waits for them, and re-layouts  14.5 us (1%)
    psum x2, waiting for transfers between devices, broadcast(): return lax.psum(block, axis)  679 us
    psum x1, waiting for transfers between devices, per_device(): weight_grad = lax.psum(grad_term, ('nodes', 'feat'))  441 us
  transfers between devices with their start and end apart: 4, of which 3 were waited for; matrix products, arithmetic and copies ran while one was open for 1% of the time, Pallas kernels for 0%

commit v1 on v0

v1 whole, which is shorter than its diff:
```python
import functools

import jax
import jax.numpy as jnp
from jax import lax
from jax.experimental import pallas as pl
from jax.experimental.pallas import tpu as pltpu
from jax.sharding import PartitionSpec as P

KL, KH, K = 2, 8, 122
BLK, HID = 128, 256
MESH = pl.DeviceIdType.MESH
A = pl.ds(0, 16)
ROWS = (pl.ds(16, 48), pl.ds(64, 64))
ALL = slice(None)
LAST = 8
LAG = 2
SCALE_STEPS = 10


def where_am_i():
    n = lax.axis_index("nodes")
    return n // 8, (n // 2) % 4, n % 2, lax.axis_index("feat")


def device(z, x, c, y):
    return ((z % 16) * 8 + (x % 4) * 2 + c, y % 4)


def kernel(
    feat_ref, vals_hbm, cols_ref, counts_ref, hubs_ref, send_ref, weight_ref, grad_ref,
    layer_ref, wgrad_ref,
    G, S, S_sm, vals, frac_v, frac, index, srow, stride, W, R1, R2, Wout,
    local_sem, small_send, small_recv, a_send, a_recv, z_send, z_recv,
    one_send, one_recv, two_send, two_recv, c_send, c_recv, s_send, s_recv, r_send, r_recv,
):
    z, x, c, y = where_am_i()
    first = c == 0

    def at_u(d):
        return device(z, x + jnp.where(first, d, 0), c, y + jnp.where(first, 0, d))

    def at_v(d):
        return device(z, x + jnp.where(first, 0, d), c, y + jnp.where(first, d, 0))

    at_uv = (at_u, at_v)
    z_peer = (device(z + 1, x, c, y), device(z + 15, x, c, y))
    other = device(z, x, 1 - c, y)

    load = pltpu.make_async_copy(vals_hbm.at[0], vals, local_sem.at[0])
    load.start()
    G[0, 0, 0, 0, 0] = feat_ref[...]
    S[0, 0, 0, 0] = send_ref[...]

    barrier = pltpu.get_barrier_semaphore()
    greeted = [device(z, x + d, c, y) for d in (1, 2, 3)]
    greeted += [device(z, x, c, y + d) for d in (1, 2, 3)]
    greeted += [*z_peer, other]
    for peer in greeted:
        pl.semaphore_signal(barrier, inc=1, device_id=peer, device_id_type=MESH)
    counts = counts_ref[...].astype(jnp.float32)
    frac_v[...] = counts / jnp.sum(counts, axis=1, keepdims=True)
    pl.semaphore_wait(barrier, len(greeted))

    pending = []

    def send(src, dst, ssem, rsem, peer):
        copy = pltpu.make_async_remote_copy(
            src_ref=src, dst_ref=dst, send_sem=ssem, recv_sem=rsem,
            device_id=peer, device_id_type=MESH,
        )
        copy.start()
        pending.append(copy)
        return copy

    def arrived(copies):
        for copy in copies:
            copy.wait_recv()

    def retire(keep):
        while len(pending) > keep:
            pending.pop(0).wait_send()

    own = G.at[0, 0, 0]
    small_v = [
        send(own.at[0, 0, pl.ds(0, 64)], own.at[0, d, pl.ds(0, 64)],
             small_send.at[1, d], small_recv.at[1, d], at_v(d))
        for d in (1, 3, 2)
    ]
    small_u = [
        send(own.at[0, 0, ROWS[1]], own.at[d, 0, ROWS[1]],
             small_send.at[0, d], small_recv.at[0, d], at_u(d))
        for d in (1, 3, 2)
    ]
    frac_copy = pltpu.make_async_copy(frac_v, frac, local_sem.at[1])
    frac_copy.start()

    def strip(p, k, way, place):
        if p == 0:
            return G.at[0, k, way, place, ALL, ROWS[0]]
        return G.at[0, k, way, ALL, place, ROWS[1]]

    def slot(k, way):
        return (0, 1) if k == LAST else (k, way)

    def z_forward(p, k):
        copies = []
        for way in (0, 1):
            if k + 1 == LAST and way == 1:
                continue
            kk, ww = slot(k + 1, way)
            src = strip(p, k, way if k else 0, 0)
            copies.append(send(src, strip(p, kk, ww, 0), z_send.at[p, way, k], z_recv.at[p, way, k], z_peer[way]))
        return copies

    def a_forward(k):
        copies = []
        for way in (0, 1):
            if k + 1 == LAST and way == 0:
                continue
            kk, ww = slot(k + 1, way)
            src = G.at[0, k, way if k else 0, ALL, ALL, A]
            dst = G.at[0, kk, ww, ALL, ALL, A]
            copies.append(send(src, dst, z_send.at[2, way, k], z_recv.at[2, way, k], z_peer[way]))
        return copies

    def s_forward(k):
        copies = []
        for way in (0, 1):
            if k + 1 == LAST and way == 0:
                continue
            kk, ww = slot(k + 1, way)
            src = S.at[0, 0, k, way if k else 0]
            copies.append(send(src, S.at[0, 0, kk, ww], z_send.at[3, way, k], z_recv.at[3, way, k], z_peer[way]))
        return copies

    def pair(k):
        if k == 0:
            return 0, 0
        if k == LAST:
            return 0, 1
        return k, ALL

    def large_one(p, k):
        kk, ww = pair(k)
        return [
            send(strip(p, kk, ww, 0), strip(p, kk, ww, d), one_send.at[p, i, k], one_recv.at[p, i, k], at_uv[p](d))
            for i, d in enumerate((1, 3))
        ]

    def large_two(p, k):
        copies = []
        for i, d in enumerate((1, 3)):
            if k == 0 and i == 1 or k == LAST and i == 0:
                continue
            kk = 0 if k == LAST else k
            copies.append(
                send(strip(p, kk, i, d), strip(p, kk, i, 2), two_send.at[p, i, k], two_recv.at[p, i, k], at_uv[p](d))
            )
        return copies

    def across(k):
        kk, ww = pair(k)
        rows = pl.ds(16, 112)
        return [send(G.at[0, kk, ww, ALL, ALL, rows], G.at[1, kk, ww, ALL, ALL, rows], c_send.at[0, k], c_recv.at[0, k], other)]

    def a_across(k):
        kk, ww = pair(k)
        return [send(G.at[0, kk, ww, ALL, ALL, A], G.at[1, kk, ww, ALL, ALL, A], c_send.at[1, k], c_recv.at[1, k], other)]

    s_moves = {1: s_forward(0)}

    def base_of(p):
        away = (z - p // 8) % 16
        cell = jnp.where(away < 8, 2 * away, (33 - 2 * away) % 16)
        core = p % 2
        rel = jnp.where(core == c, 0, 1)
        along = (x - (p // 2) % 4) % 4
        base = (rel * 16 + cell) * 16 + along * jnp.where(core == 0, 4, 1)
        return base, jnp.where(core == 0, 1, 4), (rel * 4 + along) * 16 + cell

    mine = z * 8 + x * 2 + c

    def near(s, _):
        base, step, _row = base_of(mine)
        index[s] = base + ((y - cols_ref[0, s]) % 4) * step
        return 0

    def hub(s, _):
        v = cols_ref[0, s]
        base, step, _row = base_of(hubs_ref[v // 4])
        index[s] = base + ((y - v % 4) % 4) * step
        return 0

    def far(s, _):
        base, step, row = base_of(cols_ref[0, s])
        index[s] = base
        stride[s] = step
        srow[s] = row
        return 0

    lax.fori_loop(0, KL, near, 0)
    lax.fori_loop(KL, KL + KH, hub, 0)
    lax.fori_loop(KL + KH, K, far, 0)

    frac_copy.wait()
    arrived(small_v)
    z_moves = {}
    ones = {}
    twos = {}
    crossing = []
    z_moves[0, 1] = z_forward(0, 0)
    ones[0, 0] = large_one(0, 0)
    a_small = [
        send(own.at[0, ALL, A], own.at[d, ALL, A], a_send.at[d], a_recv.at[d], at_u(d)) for d in (1, 3, 2)
    ]
    arrived(small_u)
    z_moves[1, 1] = z_forward(1, 0)
    ones[1, 0] = large_one(1, 0)
    load.wait()

    def scale(part):
        def one(s, _):
            vals[s] = (frac[0, s] * vals[s].astype(jnp.float32)).astype(jnp.bfloat16)
            return 0

        per = (K + SCALE_STEPS - 1) // SCALE_STEPS
        if part < SCALE_STEPS:
            lax.fori_loop(part * per, min(K, (part + 1) * per), one, 0)

    a_moves = {}
    s_x = s_c = None
    for k in range(1, LAST + 4 + LAG):
        scale(k - 1)
        for p in (0, 1):
            if k <= LAST:
                arrived(z_moves[p, k])
                if k < LAST:
                    z_moves[p, k + 1] = z_forward(p, k)
                ones[p, k] = large_one(p, k)
        if k <= LAST:
            arrived(s_moves[k])
            if k < LAST:
                s_moves[k + 1] = s_forward(k)
            else:
                s_x = [
                    send(S.at[0, 0], S.at[0, d], s_send.at[d], s_recv.at[d], device(z, x + d, c, y))
                    for d in (1, 2, 3)
                ]
        for p in (0, 1):
            if k - 1 <= LAST:
                arrived(ones[p, k - 1])
                twos[p, k - 1] = large_two(p, k - 1)
        step = k - LAG
        if step == 0:
            arrived(a_small)
            a_moves[1] = a_forward(0)
            crossing += a_across(0)
        elif 1 <= step <= LAST:
            arrived(a_moves[step])
            if step < LAST:
                a_moves[step + 1] = a_forward(step)
            crossing += a_across(step)
        if 0 <= k - 2 <= LAST:
            arrived(twos[0, k - 2] + twos[1, k - 2])
            crossing += across(k - 2)
        if k == LAST + 1:
            arrived(s_x)
            s_c = [send(S.at[0], S.at[1], s_send.at[0], s_recv.at[0], other)]
        if k == LAST + 2:
            arrived(s_c)
            s_copy = pltpu.make_async_copy(S, S_sm, local_sem.at[2])
            s_copy.start()
        retire(48)

    s_copy.wait()

    def resolve(s, _):
        row = srow[s]
        sent = S_sm[row // 64, (row // 16) % 4, (row // 2) % 8, row % 2, 0, mine]
        index[s] = index[s] + ((y - sent) % 4) * stride[s]
        return 0

    lax.fori_loop(KL + KH, K, resolve, 0)
    arrived(crossing)

    def block(s):
        i = index[s]
        return G[i // 256, (i // 32) % 8, (i // 16) % 2, (i // 4) % 4, i % 4]

    def pair_dot(s):
        left = jnp.concatenate([vals[s], vals[s + 1]], axis=1)
        right = jnp.concatenate([block(s), block(s + 1)], axis=0)
        return jnp.dot(left, right, preferred_element_type=jnp.float32)

    def quad(i, total):
        s = i * 8
        return total + ((pair_dot(s) + pair_dot(s + 2)) + (pair_dot(s + 4) + pair_dot(s + 6)))

    total = lax.fori_loop(0, 15, quad, pair_dot(120))
    hidden = total.astype(jnp.bfloat16)
    grad = lax.dot_general(hidden, grad_ref[...], (((0,), (0,)), ((), ())), preferred_element_type=jnp.float32)
    for i in range(16):
        for h in range(2):
            W[2 * i + h] = grad[8 * i : 8 * i + 8, 128 * h : 128 * h + 128]

    def plane_peer(j):
        px, py, pc = (x + j // 8) % 4, (y + (j // 2) % 4) % 4, (c + j % 2) % 2
        return device(z, px, pc, py), px * 8 + py * 2 + pc

    def plane_copy(j, scatter):
        peer, tile = plane_peer(j)
        me = x * 8 + y * 2 + c
        src, dst = (W.at[tile], R1.at[j]) if scatter else (Wout.at[me], Wout.at[me])
        which = 0 if scatter else 2
        return pltpu.make_async_remote_copy(
            src_ref=src, dst_ref=dst, send_sem=r_send.at[which], recv_sem=r_recv.at[which],
            device_id=peer, device_id_type=MESH,
        )

    def z_copy(j):
        return pltpu.make_async_remote_copy(
            src_ref=R2.at[0], dst_ref=R2.at[j], send_sem=r_send.at[1], recv_sem=r_recv.at[1],
            device_id=device(z + j, x, c, y), device_id_type=MESH,
        )

    def start_all(make, count):
        def go(j, _):
            make(j).start()
            return 0

        lax.fori_loop(1, count, go, 0)

    def wait_all(ref, count, sem):
        part = ref.at[pl.ds(1, count - 1)]
        pltpu.make_async_copy(part, part, sem).wait()

    me = x * 8 + y * 2 + c
    start_all(functools.partial(plane_copy, scatter=True), 32)
    layer_ref[...] = jnp.dot(hidden, weight_ref[...], preferred_element_type=jnp.float32).astype(jnp.bfloat16)
    R1[0] = W[me]
    wait_all(R1, 32, r_recv.at[0])
    R2[0] = jnp.sum(R1[...], axis=0)
    start_all(z_copy, 16)
    retire(0)
    wait_all(R2, 16, r_recv.at[1])
    wait_all(R2, 16, r_send.at[1])
    Wout[me] = jnp.sum(R2[...], axis=0)
    start_all(functools.partial(plane_copy, scatter=False), 32)
    wait_all(R1, 32, r_send.at[0])
    wait_all(Wout, 32, r_recv.at[2])
    for i in range(16):
        for h in range(2):
            wgrad_ref[8 * i : 8 * i + 8, 128 * h : 128 * h + 128] = Wout[2 * i + h]
    wait_all(Wout, 32, r_send.at[2])


def per_device(features, block_vals, block_cols, block_counts, hub_parts, send_blocks, weight, grad_out):
    vmem = pl.BlockSpec(memory_space=pltpu.VMEM)
    smem = pl.BlockSpec(memory_space=pltpu.SMEM)
    dma = pltpu.SemaphoreType.DMA
    return pl.pallas_call(
        kernel,
        out_shape=(
            jax.ShapeDtypeStruct((BLK, HID), jnp.bfloat16),
            jax.ShapeDtypeStruct((BLK, HID), jnp.float32),
        ),
        in_specs=[vmem, pl.BlockSpec(memory_space=pl.ANY), smem, vmem, smem, vmem, vmem, vmem],
        out_specs=(vmem, vmem),
        scratch_shapes=[
            pltpu.VMEM((2, 8, 2, 4, 4, BLK, BLK), jnp.bfloat16),
            pltpu.VMEM((2, 4, 8, 2, 1, BLK), jnp.int32),
            pltpu.SMEM((2, 4, 8, 2, 1, BLK), jnp.int32),
            pltpu.VMEM((K, BLK, BLK), jnp.bfloat16),
            pltpu.VMEM((1, K), jnp.float32),
            pltpu.SMEM((1, K), jnp.float32),
            pltpu.SMEM((K,), jnp.int32),
            pltpu.SMEM((K,), jnp.int32),
            pltpu.SMEM((K,), jnp.int32),
            pltpu.VMEM((32, 8, BLK), jnp.float32),
            pltpu.VMEM((32, 8, BLK), jnp.float32),
            pltpu.VMEM((16, 8, BLK), jnp.float32),
            pltpu.VMEM((32, 8, BLK), jnp.float32),
            dma((3,)),
            dma((2, 4)), dma((2, 4)),
            dma((4,)), dma((4,)),
            dma((4, 2, 8)), dma((4, 2, 8)),
            dma((2, 2, 9)), dma((2, 2, 9)),
            dma((2, 2, 9)), dma((2, 2, 9)),
            dma((2, 9)), dma((2, 9)),
            dma((4,)), dma((4,)),
            dma((3,)), dma((3,)),
        ],
        compiler_params=pltpu.CompilerParams(
            collective_id=0, has_side_effects=True, vmem_limit_bytes=40 << 20
        ),
    )(features, block_vals, block_cols, block_counts, hub_parts, send_blocks, weight, grad_out)


def solution(mesh):
    placed = (
        P(("nodes", "feat"), None),
        P(("nodes", "feat"), None, None, None),
        P(("nodes", "feat"), None),
        P(("nodes", "feat"), None),
        P(),
        P(("nodes", "feat"), None),
        P(),
        P(("nodes", "feat"), None),
    )
    return jax.shard_map(
        per_device,
        mesh=mesh,
        in_specs=placed,
        out_specs=(P(("nodes", "feat"), None), P()),
        check_vma=False,
    )
```

time: 1200 us -> 106 us (0.09)
  waiting for transfers between devices: 1120 us -> 0 us
  Pallas kernels: 0 us -> 96.5 us
  starting transfers between devices: 23.2 us -> 0 us
  between operations: 15.6 us -> 0.66 us
    psum x3 -> x0, waiting for transfers between devices: 1120 us -> none  [the longest x2 679 us: broadcast(): return lax.psum(block, axis)]
    pallas_call x0 -> x1, Pallas kernels: none -> 96.5 us  [per_device(): pl.pallas_call(kernel, out_shape=(jax.ShapeDtypeStruct((BLK, HID), jnp.bf...]
    all_to_all x1 -> x0, starting transfers between devices: 23 us -> none  [per_device(): lax.all_to_all(outgoing, 'nodes', split_axis=0, concat_axis=0, tiled=True)]
  transfers between devices with their start and end apart: 4 -> 0, of which waited for: 3 -> 0; matrix products, arithmetic and copies ran while one was open for 1% -> 0% of each run, Pallas kernels for 0% -> 0%
where the time goes in v1:
time: 106 us
  Pallas kernels  96.5 us (91%)
  local copies, waits for them, and re-layouts  8.47 us (8%)
    pallas_call x1, Pallas kernels, per_device(): pl.pallas_call(kernel, out_shape=(jax.ShapeDtypeStruct((BLK, HID), jnp.bf...  96.5 us
    unnamed x18, local copies, waits for them, and re-layouts  8.47 us

profile of v1, /device:TPU:1, one launch (start us, length us, event | category | flops | bytes accessed | tf_op | source)
XLA Modules:
  0.0 105.6 jit_solution(7057379602994528156)
XLA Ops:
  0.6 0.0 copy-start
  0.6 2.1 %copy-done = bf16[1,122,128,128]{3,2,1,0:T(8,128)(2,1)S(1)} copy-done((bf16[1,122,128,128]{3,2,1,0:T(8,128)(2,1)S(1)}, bf16[1,122,128,128]{3,2,1,0:T(8,128)(2,1)}, u32[]{:S(2)}) %copy-start) | copy-done | bytes 3997720
  2.8 0.0 copy-start.1
  2.8 0.8 copy-done.1
  3.6 0.0 copy-start.2
  3.6 0.8 copy-done.2
  4.4 0.0 copy-start.3
  4.4 0.8 copy-done.3
  5.2 0.0 copy-start.4
  5.2 0.7 copy-done.4
  5.9 0.0 copy-start.5
  5.9 0.7 copy-done.5
  6.5 0.0 copy-start.6
  6.5 0.7 copy-done.6
  7.2 0.0 copy-start.7
  7.2 0.7 copy-done.7
  7.8 96.5 %shard_map.95 = (bf16[128,256]{1,0:T(8,128)(2,1)S(1)}, f32[128,256]{1,0:T(8,128)S(1)}) custom-call(bf16[128,128]{1,0:T(8,128)(2,1)S(1)} %copy-done.3, bf16[1,122,128,128]{3,2,1,0:T(8,128)(2,1)S(1)} %copy-done, s32[1,122]{1,0:T(1,128)S(1)} %copy-done.4, s32[1,122]{1,0:T(1,128)S(1)} %copy-done.5, s32[2]{0:T(128)S(1)} %copy-done.6, s32[1,128]{1,0:T(1,128)S(1)} %copy-done.7, ...), custom_call_target="tpu_custom_call" | custom-call | tf_op jit(solution)/shard_map/pallas_call | solution.py:362
  104.3 0.6 copy.12
  104.9 0.7 copy.13
Async XLA Ops:
  0.6 2.1 %copy-start = (bf16[1,122,128,128]{3,2,1,0:T(8,128)(2,1)S(1)}, bf16[1,122,128,128]{3,2,1,0:T(8,128)(2,1)}, u32[]{:S(2)}) copy-start(bf16[1,122,128,128]{3,2,1,0:T(8,128)(2,1)} %vals_hbm.1) | copy-start | bytes 11993092
  2.8 0.8 copy-start.1
  3.6 0.8 copy-start.2
  4.4 0.8 copy-start.3
  5.2 0.7 copy-start.4
  5.9 0.7 copy-start.5
  6.5 0.7 copy-start.6
  7.2 0.7 copy-start.7

commit v2 on v0

v2 whole, which is shorter than its diff:
```python
import math

import jax
import jax.numpy as jnp
from jax import lax
from jax.experimental import pallas as pl
from jax.experimental.pallas import tpu as pltpu
from jax.sharding import PartitionSpec as P

KL, KH, K = 2, 8, 122
BLK, HID = 128, 256
MESH = pl.DeviceIdType.MESH
ALL = slice(None)
A_ROWS = pl.ds(0, 16)
ROWS = (pl.ds(16, 48), pl.ds(64, 64))
HALVES = (pl.ds(0, 2), pl.ds(2, 2))
LAST = 8
A_LAG = 1
TWO_LAG = 1
ACROSS_LAG = 3
CHUNK = 16
WORK_STEPS = 8
VMEM_BYTES = 63 << 20


def where_am_i():
    n = lax.axis_index("nodes")
    return n // 8, (n // 2) % 4, n % 2, lax.axis_index("feat")


def device(z, x, c, y):
    return ((z % 16) * 8 + (x % 4) * 2 + c, y % 4)


def kernel(
    feat_hbm, vals_hbm, cols_hbm, counts_hbm, hubs_hbm, send_hbm, weight_hbm, grad_hbm,
    layer_hbm, wgrad_hbm,
    G, S, S_sm, vals, cols, counts_v, hubs, weight, grad_out, frac_v, frac, index, srow, stride,
    layer, W, R1, R2, total_tile,
    local_sem, sent_sem, small_recv, z_recv, one_recv, two_recv, c_recv, s_sent, s_recv, r_recv,
):
    z, x, c, y = where_am_i()
    first = c == 0

    def at_u(d):
        return device(z, x + jnp.where(first, d, 0), c, y + jnp.where(first, 0, d))

    def at_v(d):
        return device(z, x + jnp.where(first, 0, d), c, y + jnp.where(first, d, 0))

    at_uv = (at_u, at_v)
    z_peer = (device(z + 1, x, c, y), device(z + 15, x, c, y))
    other = device(z, x, 1 - c, y)

    barrier = pltpu.get_barrier_semaphore()
    greeted = [device(z, x + d, c, y) for d in (1, 2, 3)]
    greeted += [device(z, x, c, y + d) for d in (1, 2, 3)]
    greeted += [*z_peer, other]
    for peer in greeted:
        pl.semaphore_signal(barrier, inc=1, device_id=peer, device_id_type=MESH)

    def load(i, src, dst):
        copy = pltpu.make_async_copy(src, dst, local_sem.at[i])
        copy.start()
        return copy

    own = G.at[0, 0, 0]
    got_feat = load(0, feat_hbm, own.at[0, 0])
    got_send = load(1, send_hbm, S.at[8, 0, 0])
    got_counts = load(2, counts_hbm, counts_v)
    got_cols = load(3, cols_hbm, cols)
    got_hubs = load(4, hubs_hbm, hubs)
    got_vals = load(5, vals_hbm.at[0], vals)
    got_weight = load(6, weight_hbm, weight)
    got_grad = load(7, grad_hbm, grad_out)
    got_counts.wait()
    counts = counts_v[...].astype(jnp.float32)
    frac_v[...] = counts / jnp.sum(counts, axis=1, keepdims=True)
    got_frac = load(8, frac_v, frac)
    got_feat.wait()
    got_send.wait()
    pl.semaphore_wait(barrier, len(greeted))

    lines = G.reshape(512 * BLK, BLK)
    sent_rows = []

    def wait_rows(sem, rows):
        part = lines.at[pl.ds(0, rows)]
        pltpu.make_async_copy(part, part, sem).wait()

    def send(src, dst, sem, peer, near_core=False):
        rows = math.prod(src.shape[:-1])
        pltpu.make_async_remote_copy(
            src_ref=src, dst_ref=dst, send_sem=sent_sem.at[int(near_core)], recv_sem=sem,
            device_id=peer, device_id_type=MESH,
        ).start()
        if not near_core:
            sent_rows.append(rows)
        return sem, rows

    def arrived(group):
        wait_rows(group[0][0], sum(rows for _, rows in group))

    front = pl.ds(0, 64)
    small_v = {
        d: send(own.at[0, 0, front], own.at[0, d, front], small_recv.at[0 if d == 1 else 1], at_v(d))
        for d in (1, 3, 2)
    }
    small_u = {
        d: send(own.at[0, 0, ROWS[1]], own.at[d, 0, ROWS[1]], small_recv.at[2 if d == 1 else 3], at_u(d))
        for d in (1, 3, 2)
    }
    s_rows = []

    def s_send(i, peer, src, dst):
        pltpu.make_async_remote_copy(
            src_ref=src, dst_ref=dst, send_sem=s_sent.at[0], recv_sem=s_recv.at[i],
            device_id=peer, device_id_type=MESH,
        ).start()
        s_rows.append(math.prod(src.shape[:-2]))
        return i, s_rows[-1]

    def s_wait(sem, rows):
        part = S.reshape(128, 1, BLK).at[pl.ds(0, rows)]
        pltpu.make_async_copy(part, part, sem).wait()

    def s_arrived(group):
        s_wait(s_recv.at[group[0][0]], sum(rows for _, rows in group))

    def s_shift(i, d, low, count):
        src, dst = S.at[pl.ds(8 + low, count)], S.at[pl.ds(8 + low + d, count)]
        return s_send(i, device(z + d + 16, x, c, y), src, dst)

    s_moves = [s_send(0, device(z, x + d, c, y), S.at[8, 0, 0], S.at[8, 0, d]) for d in (1, 3, 2)]

    def strip(p, k, way, place, half=ALL):
        if p == 0:
            return G.at[0, k, way, place, half, ROWS[0]]
        if p == 1:
            return G.at[0, k, way, half, place, ROWS[1]]
        return G.at[0, k, way, half, ALL, A_ROWS]

    def slot(k, way):
        return (0, 1) if k == LAST else (k, way)

    def z_forward(p, k, h):
        copies = []
        for way in (0, 1):
            if k + 1 == LAST and way == (0 if p == 2 else 1):
                continue
            kk, ww = slot(k + 1, way)
            src = strip(p, k, way if k else 0, 0, HALVES[h])
            dst = strip(p, kk, ww, 0, HALVES[h])
            copies.append(send(src, dst, z_recv.at[p, h, k], z_peer[way]))
        return copies

    def pair(k):
        if k == 0:
            return 0, 0
        if k == LAST:
            return 0, 1
        return k, ALL

    def large_one(p, k):
        kk, ww = pair(k)
        return [
            send(strip(p, kk, ww, 0), strip(p, kk, ww, d), one_recv.at[p, k], at_uv[p](d))
            for i, d in enumerate((1, 3))
        ]

    def large_two(p, k):
        copies = []
        for i, d in enumerate((1, 3)):
            if k == 0 and i == 1 or k == LAST and i == 0:
                continue
            kk = 0 if k == LAST else k
            copies.append(
                send(strip(p, kk, i, d), strip(p, kk, i, 2), two_recv.at[k], at_uv[p](d))
            )
        return copies

    def across(k):
        kk, ww = pair(k)
        rows = pl.ds(16, 112)
        return [send(G.at[0, kk, ww, ALL, ALL, rows], G.at[1, kk, ww, ALL, ALL, rows], c_recv.at[0], other, True)]

    def a_across(k):
        kk, ww = pair(k)
        return [send(G.at[0, kk, ww, ALL, ALL, A_ROWS], G.at[1, kk, ww, ALL, ALL, A_ROWS], c_recv.at[0], other, True)]

    def base_of(p):
        away = (z - (p >> 3)) & 15
        cell = jnp.where(away < 8, 2 * away, (33 - 2 * away) & 15)
        core = p & 1
        rel = core ^ c
        along = (x - ((p >> 1) & 3)) & 3
        base = (rel * 16 + cell) * 16 + along * jnp.where(core == 0, 4, 1)
        return base, jnp.where(core == 0, 1, 4), ((away + 8) & 15) * 8 + rel * 4 + along

    mine = z * 8 + x * 2 + c

    def near(s, _):
        base, step, _row = base_of(mine)
        index[s] = base + ((y - cols[0, s]) & 3) * step
        return 0

    def hub(s, _):
        v = cols[0, s]
        base, step, _row = base_of(hubs[v >> 2])
        index[s] = base + ((y - v) & 3) * step
        return 0

    def far(s, _):
        base, step, row = base_of(cols[0, s])
        index[s] = base
        stride[s] = step
        srow[s] = row
        return 0

    def resolve(s, _):
        row = srow[s]
        sent = S_sm[row >> 3, (row >> 2) & 1, row & 3, 0, mine]
        index[s] = index[s] + ((y - sent) & 3) * stride[s]
        return 0

    def scale(s, _):
        vals[s] = (frac[0, s] * vals[s].astype(jnp.float32)).astype(jnp.bfloat16)
        return 0

    def portion(body, low, high, part, parts):
        per = (high - low + parts - 1) // parts
        if 0 <= part < parts:
            lax.fori_loop(low + part * per, min(high, low + (part + 1) * per), body, 0)

    z_moves = {}
    ones = {}
    twos = {}
    crossing = []
    arrived([small_v[1]])
    z_moves[0, 0, 1] = z_forward(0, 0, 0)
    arrived([small_v[3], small_v[2]])
    z_moves[0, 1, 1] = z_forward(0, 0, 1)
    ones[0, 0] = large_one(0, 0)
    arrived([small_u[1]])
    z_moves[1, 0, 1] = z_forward(1, 0, 0)
    arrived([small_u[3], small_u[2]])
    z_moves[1, 1, 1] = z_forward(1, 0, 1)
    ones[1, 0] = large_one(1, 0)
    a_small = [
        send(own.at[0, ALL, A_ROWS], own.at[d, ALL, A_ROWS], small_recv.at[4], at_u(d)) for d in (1, 3, 2)
    ]
    got_cols.wait()
    got_hubs.wait()
    lax.fori_loop(0, KL, near, 0)
    lax.fori_loop(KL, KL + KH, hub, 0)
    s_arrived(s_moves)
    s_moves = [s_send(1, other, S.at[8, 0], S.at[8, 1])]
    got_frac.wait()
    got_vals.wait()
    got_s = None
    for k in range(1, LAST + ACROSS_LAG + 1):
        portion(scale, 0, K, k - 1, WORK_STEPS)
        portion(far, KL + KH, K, k - 1, 4)
        portion(resolve, KL + KH, K, k - 9, 2)
        for p in (0, 1):
            if k <= LAST:
                for h in (0, 1):
                    arrived(z_moves[p, h, k])
                    if k < LAST:
                        z_moves[p, h, k + 1] = z_forward(p, k, h)
                ones[p, k] = large_one(p, k)
        step = k - A_LAG
        if step == 0:
            arrived(a_small)
            for h in (0, 1):
                z_moves[2, h, 1] = z_forward(2, 0, h)
            crossing += a_across(0)
        elif 1 <= step <= LAST:
            for h in (0, 1):
                arrived(z_moves[2, h, step])
                if step < LAST:
                    z_moves[2, h, step + 1] = z_forward(2, step, h)
            crossing += a_across(step)
        late = k - TWO_LAG
        if 0 <= late <= LAST:
            for p in (0, 1):
                arrived(ones[p, late])
                twos[p, late] = large_two(p, late)
        late = k - ACROSS_LAG
        if 0 <= late <= LAST:
            arrived(twos[0, late] + twos[1, late])
            crossing += across(late)
        if k == 1:
            s_arrived(s_moves)
            s_moves = [s_shift(2, 1, 0, 1), s_shift(2, -1, 0, 1)]
        if k == 3:
            s_arrived(s_moves)
            s_moves = [s_shift(3, 3, -1, 3), s_shift(3, -3, -1, 3)]
        if k == 5:
            s_arrived(s_moves)
            s_moves = [s_shift(4, 4, 1, 3), s_shift(4, -4, -4, 4)]
        if k == 7:
            s_arrived(s_moves)
            got_s = load(9, S, S_sm)
        if k == 8:
            got_s.wait()

    arrived(crossing)

    flat = G.reshape(512, BLK, BLK)

    def chunk_dot(s, count):
        left = jnp.concatenate([vals[s + i] for i in range(count)], axis=1)
        right = jnp.concatenate([flat[index[s + i]] for i in range(count)], axis=0)
        return jnp.dot(left, right, preferred_element_type=jnp.float32)

    rest = K % CHUNK
    total = lax.fori_loop(
        0, K // CHUNK, lambda i, acc: acc + chunk_dot(i * CHUNK, CHUNK), chunk_dot(K - rest, rest)
    )
    hidden = total.astype(jnp.bfloat16)
    got_grad.wait()
    grad = lax.dot_general(hidden, grad_out[...], (((0,), (0,)), ((), ())), preferred_element_type=jnp.float32)
    for i in range(16):
        for h in range(2):
            W[2 * i + h] = grad[8 * i : 8 * i + 8, 128 * h : 128 * h + 128]

    me = x * 8 + y * 2 + c
    plane = sorted(
        ((dx, dy, dc) for dx in range(4) for dy in range(4) for dc in range(2) if (dx, dy, dc) != (0, 0, 0)),
        key=lambda d: -(min(d[0], 4 - d[0]) + min(d[1], 4 - d[1])) * 2 - d[2],
    )

    def at_tile(tile):
        rows = pl.ds(pl.multiple_of(8 * (tile // 2), 8), 8)
        return wgrad_hbm.at[rows, pl.ds(pl.multiple_of(BLK * (tile % 2), BLK), BLK)]

    def tile_send(src, dst, sem, peer):
        pltpu.make_async_remote_copy(
            src_ref=src, dst_ref=dst, send_sem=sent_sem.at[0], recv_sem=sem,
            device_id=peer, device_id_type=MESH,
        ).start()
        sent_rows.append(16)

    def plane_send(scatter):
        for j, (dx, dy, dc) in enumerate(plane):
            px, py, pc = (x + dx) % 4, (y + dy) % 4, (c + dc) % 2
            peer = device(z, px, pc, py)
            if scatter:
                tile_send(W.at[px * 8 + py * 2 + pc], R1.at[j + 1], r_recv.at[0], peer)
            else:
                tile_send(total_tile, at_tile(me), r_recv.at[2], peer)

    def wait_tiles(sem, count):
        part = W.at[pl.ds(0, count)]
        pltpu.make_async_copy(part, part, sem).wait()

    plane_send(True)
    got_weight.wait()
    layer[...] = jnp.dot(hidden, weight[...], preferred_element_type=jnp.float32).astype(jnp.bfloat16)
    put_layer = load(0, layer, layer_hbm)
    R1[0] = W[me]
    wait_tiles(r_recv.at[0], 31)
    R2[0] = jnp.sum(R1[...], axis=0)
    for j in (8, 7, 9, 6, 10, 5, 11, 4, 12, 3, 13, 2, 14, 1, 15):
        tile_send(R2.at[0], R2.at[j], r_recv.at[1], device(z + j, x, c, y))
    s_wait(s_sent.at[0], sum(s_rows))
    put_layer.wait()
    wait_tiles(r_recv.at[1], 15)
    total_tile[...] = jnp.sum(R2[...], axis=0)
    plane_send(False)
    put_tile = load(1, total_tile, at_tile(me))
    put_tile.wait()
    wait_tiles(r_recv.at[2], 31)
    wait_rows(sent_sem.at[0], sum(sent_rows))
    wait_rows(sent_sem.at[1], sum(rows for _, rows in crossing))


def per_device(features, block_vals, block_cols, block_counts, hub_parts, send_blocks, weight, grad_out):
    dma = pltpu.SemaphoreType.DMA
    return pl.pallas_call(
        kernel,
        out_shape=(
            jax.ShapeDtypeStruct((BLK, HID), jnp.bfloat16),
            jax.ShapeDtypeStruct((BLK, HID), jnp.float32),
        ),
        in_specs=[pl.BlockSpec(memory_space=pl.ANY)] * 8,
        out_specs=(pl.BlockSpec(memory_space=pl.ANY),) * 2,
        scratch_shapes=[
            pltpu.VMEM((2, 8, 2, 4, 4, BLK, BLK), jnp.bfloat16),
            pltpu.VMEM((16, 2, 4, 1, BLK), jnp.int32),
            pltpu.SMEM((16, 2, 4, 1, BLK), jnp.int32),
            pltpu.VMEM((K, BLK, BLK), jnp.bfloat16),
            pltpu.SMEM((1, K), jnp.int32),
            pltpu.VMEM((1, K), jnp.int32),
            pltpu.SMEM((2,), jnp.int32),
            pltpu.VMEM((BLK, HID), jnp.bfloat16),
            pltpu.VMEM((BLK, HID), jnp.bfloat16),
            pltpu.VMEM((1, K), jnp.float32),
            pltpu.SMEM((1, K), jnp.float32),
            pltpu.SMEM((K,), jnp.int32),
            pltpu.SMEM((K,), jnp.int32),
            pltpu.SMEM((K,), jnp.int32),
            pltpu.VMEM((BLK, HID), jnp.bfloat16),
            pltpu.VMEM((32, 8, BLK), jnp.float32),
            pltpu.VMEM((32, 8, BLK), jnp.float32),
            pltpu.VMEM((16, 8, BLK), jnp.float32),
            pltpu.VMEM((8, BLK), jnp.float32),
            dma((10,)), dma((2,)), dma((5,)), dma((3, 2, 9)), dma((2, 9)), dma((9,)),
            dma((1,)), dma((1,)), dma((5,)), dma((3,)),
        ],
        compiler_params=pltpu.CompilerParams(
            collective_id=0, has_side_effects=True, vmem_limit_bytes=VMEM_BYTES
        ),
    )(features, block_vals, block_cols, block_counts, hub_parts, send_blocks, weight, grad_out)


def solution(mesh):
    placed = (
        P(("nodes", "feat"), None),
        P(("nodes", "feat"), None, None, None),
        P(("nodes", "feat"), None),
        P(("nodes", "feat"), None),
        P(),
        P(("nodes", "feat"), None),
        P(),
        P(("nodes", "feat"), None),
    )
    return jax.shard_map(
        per_device,
        mesh=mesh,
        in_specs=placed,
        out_specs=(P(("nodes", "feat"), None), P()),
        check_vma=False,
    )
```

time: 1200 us -> 84.5 us (0.07)
  waiting for transfers between devices: 1120 us -> 0 us
  Pallas kernels: 0 us -> 80.6 us
  starting transfers between devices: 23.2 us -> 0 us
  between operations: 15.6 us -> 0.64 us
    psum x3 -> x0, waiting for transfers between devices: 1120 us -> none  [the longest x2 679 us: broadcast(): return lax.psum(block, axis)]
    pallas_call x0 -> x1, Pallas kernels: none -> 80.6 us  [per_device(): pl.pallas_call(kernel, out_shape=(jax.ShapeDtypeStruct((BLK, HID), jnp.bf...]
    all_to_all x1 -> x0, starting transfers between devices: 23 us -> none  [per_device(): lax.all_to_all(outgoing, 'nodes', split_axis=0, concat_axis=0, tiled=True)]
  transfers between devices with their start and end apart: 4 -> 0, of which waited for: 3 -> 0; matrix products, arithmetic and copies ran while one was open for 1% -> 0% of each run, Pallas kernels for 0% -> 0%
where the time goes in v2:
time: 84.5 us; the launch traced here: 84.3 us
  Pallas kernels  80.6 us (95%)
  local copies, waits for them, and re-layouts  3.04 us (4%)
    pallas_call x1, Pallas kernels, per_device(): pl.pallas_call(kernel, out_shape=(jax.ShapeDtypeStruct((BLK, HID), jnp.bf...  80.6 us
    unnamed x2, local copies, waits for them, and re-layouts  3.04 us

profile of v2, /device:TPU:1, one launch (start us, length us, event | category | flops | bytes accessed | tf_op | source)
XLA Modules:
  0.0 84.3 jit_solution(10320102391272458984)
XLA Ops:
  0.6 80.6 %shard_map.95 = (bf16[128,256]{1,0:T(8,128)(2,1)}, f32[128,256]{1,0:T(8,128)}) custom-call(bf16[128,128]{1,0:T(8,128)(2,1)} %feat_hbm.1, bf16[1,122,128,128]{3,2,1,0:T(8,128)(2,1)} %vals_hbm.1, s32[1,122]{1,0:T(1,128)} %cols_hbm.1, s32[1,122]{1,0:T(1,128)} %counts_hbm.1, s32[2]{0:T(128)} %hubs_hbm.1, s32[1,128]{1,0:T(1,128)} %send_hbm.1, ...), custom_call_target="tpu_custom_call" | custom-call | tf_op jit(solution)/shard_map/pallas_call | solution.py:381
  81.2 1.5 %copy.12 = bf16[128,256]{1,0:T(8,128)(2,1)} copy(bf16[128,256]{1,0:T(8,128)(2,1)} %get-tuple-element.4) | data formatting | bytes 131072
  82.7 1.6 %copy.13 = f32[128,256]{1,0:T(8,128)} copy(f32[128,256]{1,0:T(8,128)} %get-tuple-element.5) | data formatting | bytes 262144

commit v3 on v2

--- a/solution.py
+++ b/solution.py
@@ -16,9 +16,9 @@
 HALVES = (pl.ds(0, 2), pl.ds(2, 2))
 LAST = 8
 A_LAG = 1
-TWO_LAG = 1
-ACROSS_LAG = 3
-CHUNK = 16
+ACROSS_LAG = 2
+DIRECT = (LAST,)
+CHUNK = 61
 WORK_STEPS = 8
 VMEM_BYTES = 63 << 20
 
@@ -36,7 +36,7 @@
     feat_hbm, vals_hbm, cols_hbm, counts_hbm, hubs_hbm, send_hbm, weight_hbm, grad_hbm,
     layer_hbm, wgrad_hbm,
     G, S, S_sm, vals, cols, counts_v, hubs, weight, grad_out, frac_v, frac, index, srow, stride,
-    layer, W, R1, R2, total_tile,
+    layer, W, R1, R2, total_strip,
     local_sem, sent_sem, small_recv, z_recv, one_recv, two_recv, c_recv, s_sent, s_recv, r_recv,
 ):
     z, x, c, y = where_am_i()
@@ -73,12 +73,6 @@
     got_vals = load(5, vals_hbm.at[0], vals)
     got_weight = load(6, weight_hbm, weight)
     got_grad = load(7, grad_hbm, grad_out)
-    got_counts.wait()
-    counts = counts_v[...].astype(jnp.float32)
-    frac_v[...] = counts / jnp.sum(counts, axis=1, keepdims=True)
-    got_frac = load(8, frac_v, frac)
-    got_feat.wait()
-    got_send.wait()
     pl.semaphore_wait(barrier, len(greeted))
 
     lines = G.reshape(512 * BLK, BLK)
@@ -103,13 +97,14 @@
 
     front = pl.ds(0, 64)
     small_v = {
-        d: send(own.at[0, 0, front], own.at[0, d, front], small_recv.at[0 if d == 1 else 1], at_v(d))
+        d: send(feat_hbm.at[front], own.at[0, d, front], small_recv.at[0 if d == 1 else 1], at_v(d))
         for d in (1, 3, 2)
     }
     small_u = {
-        d: send(own.at[0, 0, ROWS[1]], own.at[d, 0, ROWS[1]], small_recv.at[2 if d == 1 else 3], at_u(d))
+        d: send(feat_hbm.at[ROWS[1]], own.at[d, 0, ROWS[1]], small_recv.at[2 if d == 1 else 3], at_u(d))
         for d in (1, 3, 2)
     }
+    got_send.wait()
     s_rows = []
 
     def s_send(i, peer, src, dst):
@@ -161,32 +156,36 @@
             return 0, 1
         return k, ALL
 
-    def large_one(p, k):
+    def large_one(p, k, h):
         kk, ww = pair(k)
+        half = HALVES[h] if k else ALL
         return [
-            send(strip(p, kk, ww, 0), strip(p, kk, ww, d), one_recv.at[p, k], at_uv[p](d))
-            for i, d in enumerate((1, 3))
+            send(strip(p, kk, ww, 0, half), strip(p, kk, ww, d, half), one_recv.at[p, h, k], at_uv[p](d))
+            for d in ((1, 3, 2) if k in DIRECT else (1, 3))
         ]
 
-    def large_two(p, k):
+    def large_two(p, k, h):
         copies = []
+        if k in DIRECT:
+            return copies
+        half = HALVES[h] if k else ALL
         for i, d in enumerate((1, 3)):
             if k == 0 and i == 1 or k == LAST and i == 0:
                 continue
             kk = 0 if k == LAST else k
-            copies.append(
-                send(strip(p, kk, i, d), strip(p, kk, i, 2), two_recv.at[k], at_uv[p](d))
-            )
+            copies.append(send(strip(p, kk, i, d, half), strip(p, kk, i, 2, half), two_recv.at[k], at_uv[p](d)))
         return copies
 
-    def across(k):
+    def across(part):
+        return [send(G.at[(0, *part)], G.at[(1, *part)], c_recv.at[0], other, True)]
+
+    def rest_across(k):
         kk, ww = pair(k)
-        rows = pl.ds(16, 112)
-        return [send(G.at[0, kk, ww, ALL, ALL, rows], G.at[1, kk, ww, ALL, ALL, rows], c_recv.at[0], other, True)]
+        return across((kk, ww, ALL, ALL, pl.ds(16, 112)))
 
     def a_across(k):
         kk, ww = pair(k)
-        return [send(G.at[0, kk, ww, ALL, ALL, A_ROWS], G.at[1, kk, ww, ALL, ALL, A_ROWS], c_recv.at[0], other, True)]
+        return across((kk, ww, ALL, ALL, A_ROWS))
 
     def base_of(p):
         away = (z - (p >> 3)) & 15
@@ -236,19 +235,22 @@
     ones = {}
     twos = {}
     crossing = []
+    got_counts.wait()
+    counts = counts_v[...].astype(jnp.float32)
+    frac_v[...] = counts / jnp.sum(counts, axis=1, keepdims=True)
+    got_frac = load(8, frac_v, frac)
+    got_feat.wait()
     arrived([small_v[1]])
     z_moves[0, 0, 1] = z_forward(0, 0, 0)
+    arrived([small_u[1]])
+    z_moves[1, 0, 1] = z_forward(1, 0, 0)
     arrived([small_v[3], small_v[2]])
     z_moves[0, 1, 1] = z_forward(0, 0, 1)
-    ones[0, 0] = large_one(0, 0)
-    arrived([small_u[1]])
-    z_moves[1, 0, 1] = z_forward(1, 0, 0)
+    ones[0, 0, 0] = large_one(0, 0, 0)
+    a_small = [send(own.at[0, ALL, A_ROWS], own.at[d, ALL, A_ROWS], small_recv.at[4], at_u(d)) for d in (1, 3, 2)]
     arrived([small_u[3], small_u[2]])
     z_moves[1, 1, 1] = z_forward(1, 0, 1)
-    ones[1, 0] = large_one(1, 0)
-    a_small = [
-        send(own.at[0, ALL, A_ROWS], own.at[d, ALL, A_ROWS], small_recv.at[4], at_u(d)) for d in (1, 3, 2)
-    ]
+    ones[1, 0, 0] = large_one(1, 0, 0)
     got_cols.wait()
     got_hubs.wait()
     lax.fori_loop(0, KL, near, 0)
@@ -258,38 +260,47 @@
     got_frac.wait()
     got_vals.wait()
     got_s = None
+
+    def z_step(p, h, k):
+        if 1 <= k <= LAST:
+            arrived(z_moves[p, h, k])
+            if k < LAST:
+                z_moves[p, h, k + 1] = z_forward(p, k, h)
+            if p < 2:
+                ones[p, h, k] = large_one(p, k, h)
+
+    def plane_step(p, h, k):
+        if (p, h, k) in ones:
+            arrived(ones[p, h, k])
+            twos.setdefault(k, []).extend(large_two(p, k, h))
+
     for k in range(1, LAST + ACROSS_LAG + 1):
         portion(scale, 0, K, k - 1, WORK_STEPS)
         portion(far, KL + KH, K, k - 1, 4)
         portion(resolve, KL + KH, K, k - 9, 2)
-        for p in (0, 1):
-            if k <= LAST:
-                for h in (0, 1):
-                    arrived(z_moves[p, h, k])
-                    if k < LAST:
-                        z_moves[p, h, k + 1] = z_forward(p, k, h)
-                ones[p, k] = large_one(p, k)
+        z_step(0, 0, k)
+        z_step(1, 0, k)
+        plane_step(0, 0, k - 1)
+        plane_step(1, 0, k - 1)
+        z_step(0, 1, k)
+        plane_step(0, 1, k - 1)
+        z_step(1, 1, k)
+        plane_step(1, 1, k - 1)
+        late = k - ACROSS_LAG
+        if 0 <= late <= LAST and late not in DIRECT:
+            arrived(twos[late])
+            crossing += rest_across(late)
+        if k - 1 in DIRECT:
+            crossing += rest_across(k - 1)
         step = k - A_LAG
         if step == 0:
             arrived(a_small)
-            for h in (0, 1):
-                z_moves[2, h, 1] = z_forward(2, 0, h)
-            crossing += a_across(0)
-        elif 1 <= step <= LAST:
-            for h in (0, 1):
-                arrived(z_moves[2, h, step])
-                if step < LAST:
-                    z_moves[2, h, step + 1] = z_forward(2, step, h)
+            z_moves[2, 0, 1] = z_forward(2, 0, 0)
+            z_moves[2, 1, 1] = z_forward(2, 0, 1)
+        z_step(2, 0, step)
+        z_step(2, 1, step)
+        if 0 <= step <= LAST:
             crossing += a_across(step)
-        late = k - TWO_LAG
-        if 0 <= late <= LAST:
-            for p in (0, 1):
-                arrived(ones[p, late])
-                twos[p, late] = large_two(p, late)
-        late = k - ACROSS_LAG
-        if 0 <= late <= LAST:
-            arrived(twos[0, late] + twos[1, late])
-            crossing += across(late)
         if k == 1:
             s_arrived(s_moves)
             s_moves = [s_shift(2, 1, 0, 1), s_shift(2, -1, 0, 1)]
@@ -314,78 +325,109 @@
         right = jnp.concatenate([flat[index[s + i]] for i in range(count)], axis=0)
         return jnp.dot(left, right, preferred_element_type=jnp.float32)
 
-    rest = K % CHUNK
-    total = lax.fori_loop(
-        0, K // CHUNK, lambda i, acc: acc + chunk_dot(i * CHUNK, CHUNK), chunk_dot(K - rest, rest)
-    )
+    total = lax.fori_loop(1, K // CHUNK, lambda i, acc: acc + chunk_dot(i * CHUNK, CHUNK), chunk_dot(0, CHUNK))
     hidden = total.astype(jnp.bfloat16)
     got_grad.wait()
     grad = lax.dot_general(hidden, grad_out[...], (((0,), (0,)), ((), ())), preferred_element_type=jnp.float32)
     for i in range(16):
-        for h in range(2):
-            W[2 * i + h] = grad[8 * i : 8 * i + 8, 128 * h : 128 * h + 128]
-
-    me = x * 8 + y * 2 + c
+        W[i] = grad[8 * i : 8 * i + 8]
+
+    me = x * 4 + y
+    owner = c == 1
     plane = sorted(
-        ((dx, dy, dc) for dx in range(4) for dy in range(4) for dc in range(2) if (dx, dy, dc) != (0, 0, 0)),
-        key=lambda d: -(min(d[0], 4 - d[0]) + min(d[1], 4 - d[1])) * 2 - d[2],
+        ((dx, dy) for dx in range(4) for dy in range(4)),
+        key=lambda d: -min(d[0], 4 - d[0]) - min(d[1], 4 - d[1]),
     )
 
-    def at_tile(tile):
-        rows = pl.ds(pl.multiple_of(8 * (tile // 2), 8), 8)
-        return wgrad_hbm.at[rows, pl.ds(pl.multiple_of(BLK * (tile % 2), BLK), BLK)]
-
-    def tile_send(src, dst, sem, peer):
+    def at_strip(i):
+        return wgrad_hbm.at[pl.ds(pl.multiple_of(8 * i, 8), 8)]
+
+    def strip_send(src, dst, sem, peer):
         pltpu.make_async_remote_copy(
-            src_ref=src, dst_ref=dst, send_sem=sent_sem.at[0], recv_sem=sem,
+            src_ref=src, dst_ref=dst, send_sem=sent_sem.at[2], recv_sem=sem,
             device_id=peer, device_id_type=MESH,
         ).start()
-        sent_rows.append(16)
-
-    def plane_send(scatter):
-        for j, (dx, dy, dc) in enumerate(plane):
-            px, py, pc = (x + dx) % 4, (y + dy) % 4, (c + dc) % 2
-            peer = device(z, px, pc, py)
-            if scatter:
-                tile_send(W.at[px * 8 + py * 2 + pc], R1.at[j + 1], r_recv.at[0], peer)
-            else:
-                tile_send(total_tile, at_tile(me), r_recv.at[2], peer)
-
-    def wait_tiles(sem, count):
-        part = W.at[pl.ds(0, count)]
-        pltpu.make_async_copy(part, part, sem).wait()
-
-    plane_send(True)
+
+    def wait_strips(sem, count):
+        wait_rows(sem, 32 * count)
+
+    for j, (dx, dy) in enumerate(plane):
+        px, py = (x + dx) % 4, (y + dy) % 4
+
+        def scatter(px=px, py=py, j=j):
+            strip_send(W.at[px * 4 + py], R1.at[2 * j + c], r_recv.at[0], device(z, px, 1, py))
+
+        if dx or dy:
+            scatter()
+        else:
+            pl.when(c == 0)(scatter)
+
+    @pl.when(owner)
+    def _():
+        R1[31] = W[me]
+        wait_strips(r_recv.at[0], 31)
+        R2[0] = jnp.sum(R1[...], axis=0)
+        for j in (8, 7, 9, 6, 10, 5, 11, 4, 12, 3, 13, 2, 14, 1, 15):
+            strip_send(R2.at[0], R2.at[j], r_recv.at[1], device(z + j, x, c, y))
+
     got_weight.wait()
     layer[...] = jnp.dot(hidden, weight[...], preferred_element_type=jnp.float32).astype(jnp.bfloat16)
     put_layer = load(0, layer, layer_hbm)
-    R1[0] = W[me]
-    wait_tiles(r_recv.at[0], 31)
-    R2[0] = jnp.sum(R1[...], axis=0)
-    for j in (8, 7, 9, 6, 10, 5, 11, 4, 12, 3, 13, 2, 14, 1, 15):
-        tile_send(R2.at[0], R2.at[j], r_recv.at[1], device(z + j, x, c, y))
     s_wait(s_sent.at[0], sum(s_rows))
-    put_layer.wait()
-    wait_tiles(r_recv.at[1], 15)
-    total_tile[...] = jnp.sum(R2[...], axis=0)
-    plane_send(False)
-    put_tile = load(1, total_tile, at_tile(me))
-    put_tile.wait()
-    wait_tiles(r_recv.at[2], 31)
     wait_rows(sent_sem.at[0], sum(sent_rows))
     wait_rows(sent_sem.at[1], sum(rows for _, rows in crossing))
+    put_layer.wait()
+
+    @pl.when(owner)
+    def _():
+        wait_strips(r_recv.at[1], 15)
+        total_strip[...] = jnp.sum(R2[...], axis=0)
+        for dx, dy in plane:
+            px, py = (x + dx) % 4, (y + dy) % 4
+            strip_send(total_strip, at_strip(me), r_recv.at[2], device(z, px, 0, py))
+            if dx or dy:
+                strip_send(total_strip, at_strip(me), r_recv.at[2], device(z, px, 1, py))
+        put_strip = load(1, total_strip, at_strip(me))
+        put_strip.wait()
+        wait_strips(r_recv.at[2], 15)
+        wait_strips(sent_sem.at[2], 15 + 15 + 31)
+
+    @pl.when(c == 0)
+    def _():
+        wait_strips(r_recv.at[2], 16)
+        wait_strips(sent_sem.at[2], 16)
+
+
+def hand_over(layer_from, wgrad_from, layer_to, wgrad_to, layer, wgrad, sem):
+    fetch = [
+        pltpu.make_async_copy(layer_from, layer, sem.at[0]),
+        pltpu.make_async_copy(wgrad_from, wgrad, sem.at[1]),
+    ]
+    store = [
+        pltpu.make_async_copy(layer, layer_to, sem.at[2]),
+        pltpu.make_async_copy(wgrad, wgrad_to, sem.at[3]),
+    ]
+    for copy in fetch:
+        copy.start()
+    for copy, then in zip(fetch, store):
+        copy.wait()
+        then.start()
+    for copy in store:
+        copy.wait()
 
 
 def per_device(features, block_vals, block_cols, block_counts, hub_parts, send_blocks, weight, grad_out):
     dma = pltpu.SemaphoreType.DMA
-    return pl.pallas_call(
+    anywhere = pl.BlockSpec(memory_space=pl.ANY)
+    outs = (
+        jax.ShapeDtypeStruct((BLK, HID), jnp.bfloat16),
+        jax.ShapeDtypeStruct((BLK, HID), jnp.float32),
+    )
+    results = pl.pallas_call(
         kernel,
-        out_shape=(
-            jax.ShapeDtypeStruct((BLK, HID), jnp.bfloat16),
-            jax.ShapeDtypeStruct((BLK, HID), jnp.float32),
-        ),
-        in_specs=[pl.BlockSpec(memory_space=pl.ANY)] * 8,
-        out_specs=(pl.BlockSpec(memory_space=pl.ANY),) * 2,
+        out_shape=outs,
+        in_specs=[anywhere] * 8,
+        out_specs=(anywhere,) * 2,
         scratch_shapes=[
             pltpu.VMEM((2, 8, 2, 4, 4, BLK, BLK), jnp.bfloat16),
             pltpu.VMEM((16, 2, 4, 1, BLK), jnp.int32),
@@ -402,17 +444,25 @@
             pltpu.SMEM((K,), jnp.int32),
             pltpu.SMEM((K,), jnp.int32),
             pltpu.VMEM((BLK, HID), jnp.bfloat16),
-            pltpu.VMEM((32, 8, BLK), jnp.float32),
-            pltpu.VMEM((32, 8, BLK), jnp.float32),
-            pltpu.VMEM((16, 8, BLK), jnp.float32),
-            pltpu.VMEM((8, BLK), jnp.float32),
-            dma((10,)), dma((2,)), dma((5,)), dma((3, 2, 9)), dma((2, 9)), dma((9,)),
+            pltpu.VMEM((16, 8, HID), jnp.float32),
+            pltpu.VMEM((32, 8, HID), jnp.float32),
+            pltpu.VMEM((16, 8, HID), jnp.float32),
+            pltpu.VMEM((8, HID), jnp.float32),
+            dma((10,)), dma((3,)), dma((5,)), dma((3, 2, 9)), dma((2, 2, 9)), dma((9,)),
             dma((1,)), dma((1,)), dma((5,)), dma((3,)),
         ],
         compiler_params=pltpu.CompilerParams(
             collective_id=0, has_side_effects=True, vmem_limit_bytes=VMEM_BYTES
         ),
     )(features, block_vals, block_cols, block_counts, hub_parts, send_blocks, weight, grad_out)
+    return pl.pallas_call(
+        hand_over,
+        out_shape=outs,
+        in_specs=[anywhere] * 2,
+        out_specs=(anywhere,) * 2,
+        scratch_shapes=[pltpu.VMEM((BLK, HID), jnp.bfloat16), pltpu.VMEM((BLK, HID), jnp.float32), dma((4,))],
+        compiler_params=pltpu.CompilerParams(vmem_limit_bytes=VMEM_BYTES),
+    )(*results)
 
 
 def solution(mesh):

time: 84.5 us -> 79.4 us (0.940)
  local copies, waits for them, and re-layouts: 3.04 us -> 0 us
  Pallas kernels: 80.6 us -> 78.6 us
    unnamed x2 -> x0, local copies, waits for them, and re-layouts: 3.04 us -> none
    pallas_call x1 -> x2, Pallas kernels: 80.6 us -> 78.6 us  [the longest x1 77 us: per_device(): pl.pallas_call(kernel, out_shape=outs, in_specs=[anywhere] * 8, out_specs...]
where the time goes in v3:
time: 79.4 us; the launch traced here: 79.2 us
  Pallas kernels  78.6 us (99%)
    pallas_call x1, Pallas kernels, per_device(): pl.pallas_call(kernel, out_shape=outs, in_specs=[anywhere] * 8, out_specs...  77 us
    pallas_call x1, Pallas kernels, per_device(): pl.pallas_call(hand_over, out_shape=outs, in_specs=[anywhere] * 2, out_sp...  1.63 us

profile of v3, /device:TPU:1, one launch (start us, length us, event | category | flops | bytes accessed | tf_op | source)
XLA Modules:
  0.0 79.2 jit_solution(12431299581679049203)
XLA Ops:
  0.6 77.0 %shard_map.95 = (bf16[128,256]{1,0:T(8,128)(2,1)}, f32[128,256]{1,0:T(8,128)}) custom-call(bf16[128,128]{1,0:T(8,128)(2,1)} %feat_hbm.1, bf16[1,122,128,128]{3,2,1,0:T(8,128)(2,1)} %vals_hbm.1, s32[1,122]{1,0:T(1,128)} %cols_hbm.1, s32[1,122]{1,0:T(1,128)} %counts_hbm.1, s32[2]{0:T(128)} %hubs_hbm.1, s32[1,128]{1,0:T(1,128)} %send_hbm.1, ...), custom_call_target="tpu_custom_call" | custom-call | tf_op jit(solution)/shard_map/pallas_call | solution.py:426
  77.6 1.6 %shard_map.96 = (bf16[128,256]{1,0:T(8,128)(2,1)}, f32[128,256]{1,0:T(8,128)}) custom-call(bf16[128,256]{1,0:T(8,128)(2,1)} %get-tuple-element.4.layer_from, f32[128,256]{1,0:T(8,128)} %get-tuple-element.5.wgrad_from), custom_call_target="tpu_custom_call" | custom-call | tf_op jit(solution)/shard_map/pallas_call | solution.py:458

commit v4 on v3

--- a/solution.py
+++ b/solution.py
@@ -18,8 +18,9 @@
 A_LAG = 1
 ACROSS_LAG = 2
 DIRECT = (LAST,)
+SPLIT = (LAST - 1,)
 CHUNK = 61
-WORK_STEPS = 8
+WORK_STEPS = 6
 VMEM_BYTES = 63 << 20
 
 
@@ -179,7 +180,21 @@
     def across(part):
         return [send(G.at[(0, *part)], G.at[(1, *part)], c_recv.at[0], other, True)]
 
+    def places_across(k, *places):
+        kk, ww = pair(k)
+        copies = []
+        for place in places:
+            copies += across((kk, ww, place, ALL, ROWS[0])) + across((kk, ww, ALL, place, ROWS[1]))
+        return copies
+
+    def last_across(p, h):
+        if p == 0:
+            return across((0, 1, ALL, HALVES[h], ROWS[0]))
+        return across((0, 1, HALVES[h], ALL, ROWS[1]))
+
     def rest_across(k):
+        if k in SPLIT:
+            return places_across(k, 2)
         kk, ww = pair(k)
         return across((kk, ww, ALL, ALL, pl.ds(16, 112)))
 
@@ -251,14 +266,8 @@
     arrived([small_u[3], small_u[2]])
     z_moves[1, 1, 1] = z_forward(1, 0, 1)
     ones[1, 0, 0] = large_one(1, 0, 0)
-    got_cols.wait()
-    got_hubs.wait()
-    lax.fori_loop(0, KL, near, 0)
-    lax.fori_loop(KL, KL + KH, hub, 0)
     s_arrived(s_moves)
     s_moves = [s_send(1, other, S.at[8, 0], S.at[8, 1])]
-    got_frac.wait()
-    got_vals.wait()
     got_s = None
 
     def z_step(p, h, k):
@@ -273,10 +282,19 @@
         if (p, h, k) in ones:
             arrived(ones[p, h, k])
             twos.setdefault(k, []).extend(large_two(p, k, h))
+            if k == LAST:
+                crossing.extend(last_across(p, h))
 
     for k in range(1, LAST + ACROSS_LAG + 1):
-        portion(scale, 0, K, k - 1, WORK_STEPS)
-        portion(far, KL + KH, K, k - 1, 4)
+        if k == 3:
+            got_cols.wait()
+            got_hubs.wait()
+            got_frac.wait()
+            got_vals.wait()
+            lax.fori_loop(0, KL, near, 0)
+            lax.fori_loop(KL, KL + KH, hub, 0)
+        portion(scale, 0, K, k - 3, WORK_STEPS)
+        portion(far, KL + KH, K, k - 4, 4)
         portion(resolve, KL + KH, K, k - 9, 2)
         z_step(0, 0, k)
         z_step(1, 0, k)
@@ -290,8 +308,8 @@
         if 0 <= late <= LAST and late not in DIRECT:
             arrived(twos[late])
             crossing += rest_across(late)
-        if k - 1 in DIRECT:
-            crossing += rest_across(k - 1)
+        if k - 1 in SPLIT:
+            crossing += places_across(k - 1, pl.ds(0, 2), 3)
         step = k - A_LAG
         if step == 0:
             arrived(a_small)

time: 79.4 us -> 77.8 us (0.980)
  Pallas kernels: 78.6 us -> 77 us
    pallas_call x1, Pallas kernels: 77 us -> 75.4 us  [per_device(): pl.pallas_call(kernel, out_shape=outs, in_specs=[anywhere] * 8, out_specs...]
where the time goes in v4:
time: 77.8 us; the launch traced here: 77.7 us
  Pallas kernels  77 us (99%)
    pallas_call x1, Pallas kernels, per_device(): pl.pallas_call(kernel, out_shape=outs, in_specs=[anywhere] * 8, out_specs...  75.4 us
    pallas_call x1, Pallas kernels, per_device(): pl.pallas_call(hand_over, out_shape=outs, in_specs=[anywhere] * 2, out_sp...  1.63 us

profile of v4, /device:TPU:1, one launch (start us, length us, event | category | flops | bytes accessed | tf_op | source)
XLA Modules:
  0.0 77.7 jit_solution(9758031326085150247)
XLA Ops:
  0.6 75.4 %shard_map.95 = (bf16[128,256]{1,0:T(8,128)(2,1)}, f32[128,256]{1,0:T(8,128)}) custom-call(bf16[128,128]{1,0:T(8,128)(2,1)} %feat_hbm.1, bf16[1,122,128,128]{3,2,1,0:T(8,128)(2,1)} %vals_hbm.1, s32[1,122]{1,0:T(1,128)} %cols_hbm.1, s32[1,122]{1,0:T(1,128)} %counts_hbm.1, s32[2]{0:T(128)} %hubs_hbm.1, s32[1,128]{1,0:T(1,128)} %send_hbm.1, ...), custom_call_target="tpu_custom_call" | custom-call | tf_op jit(solution)/shard_map/pallas_call | solution.py:444
  76.0 1.6 %shard_map.96 = (bf16[128,256]{1,0:T(8,128)(2,1)}, f32[128,256]{1,0:T(8,128)}) custom-call(bf16[128,256]{1,0:T(8,128)(2,1)} %get-tuple-element.4.layer_from, f32[128,256]{1,0:T(8,128)} %get-tuple-element.5.wgrad_from), custom_call_target="tpu_custom_call" | custom-call | tf_op jit(solution)/shard_map/pallas_call | solution.py:476

commit v5 on v4

--- a/solution.py
+++ b/solution.py
@@ -19,7 +19,7 @@
 ACROSS_LAG = 2
 DIRECT = (LAST,)
 SPLIT = (LAST - 1,)
-CHUNK = 61
+CHUNK = K
 WORK_STEPS = 6
 VMEM_BYTES = 63 << 20
 
@@ -343,7 +343,7 @@
         right = jnp.concatenate([flat[index[s + i]] for i in range(count)], axis=0)
         return jnp.dot(left, right, preferred_element_type=jnp.float32)
 
-    total = lax.fori_loop(1, K // CHUNK, lambda i, acc: acc + chunk_dot(i * CHUNK, CHUNK), chunk_dot(0, CHUNK))
+    total = chunk_dot(0, CHUNK)
     hidden = total.astype(jnp.bfloat16)
     got_grad.wait()
     grad = lax.dot_general(hidden, grad_out[...], (((0,), (0,)), ((), ())), preferred_element_type=jnp.float32)
@@ -466,7 +466,7 @@
             pltpu.VMEM((32, 8, HID), jnp.float32),
             pltpu.VMEM((16, 8, HID), jnp.float32),
             pltpu.VMEM((8, HID), jnp.float32),
-            dma((10,)), dma((3,)), dma((5,)), dma((3, 2, 9)), dma((2, 2, 9)), dma((9,)),
+            dma((10,)), dma((3,)), dma((5,)), dma((3, 2, LAST)), dma((2, 2, LAST + 1)), dma((LAST,)),
             dma((1,)), dma((1,)), dma((5,)), dma((3,)),
         ],
         compiler_params=pltpu.CompilerParams(

time: 77.8 us -> 77.7 us (level)
  no operation moved by 1% of the time
where the time goes in v5:
time: 77.7 us; the launch traced here: 77.6 us
  Pallas kernels  77 us (99%)
    pallas_call x1, Pallas kernels, per_device(): pl.pallas_call(kernel, out_shape=outs, in_specs=[anywhere] * 8, out_specs...  75.3 us
    pallas_call x1, Pallas kernels, per_device(): pl.pallas_call(hand_over, out_shape=outs, in_specs=[anywhere] * 2, out_sp...  1.63 us

profile of v5, /device:TPU:1, one launch (start us, length us, event | category | flops | bytes accessed | tf_op | source)
XLA Modules:
  0.0 77.6 jit_solution(4369568909925112352)
XLA Ops:
  0.6 75.3 %shard_map.95 = (bf16[128,256]{1,0:T(8,128)(2,1)}, f32[128,256]{1,0:T(8,128)}) custom-call(bf16[128,128]{1,0:T(8,128)(2,1)} %feat_hbm.1, bf16[1,122,128,128]{3,2,1,0:T(8,128)(2,1)} %vals_hbm.1, s32[1,122]{1,0:T(1,128)} %cols_hbm.1, s32[1,122]{1,0:T(1,128)} %counts_hbm.1, s32[2]{0:T(128)} %hubs_hbm.1, s32[1,128]{1,0:T(1,128)} %send_hbm.1, ...), custom_call_target="tpu_custom_call" | custom-call | tf_op jit(solution)/shard_map/pallas_call | solution.py:444
  76.0 1.6 %shard_map.96 = (bf16[128,256]{1,0:T(8,128)(2,1)}, f32[128,256]{1,0:T(8,128)}) custom-call(bf16[128,256]{1,0:T(8,128)(2,1)} %get-tuple-element.4.layer_from, f32[128,256]{1,0:T(8,128)} %get-tuple-element.5.wgrad_from), custom_call_target="tpu_custom_call" | custom-call | tf_op jit(solution)/shard_map/pallas_call | solution.py:476
